TPU v7x, 256 devices: a whole 4x4x8 slice. The times are simulated.
256 devices in a mesh: seq: 64 (over z, x, core), head: 4 (over y).
Axes of the slice: x: 4, y: 4, z: 8, core: 2. Of those that a mesh axis runs over, the one named last changes fastest.
Arguments:
- query_key: bfloat16 [32768, 128], P('seq'), may hold values from -1.5 to 1.5
- values: bfloat16 [32768, 5120], P('seq', 'head'), may hold values from -0.119628906 to 0.119628906
- cotangent: bfloat16 [32768, 5120], P('seq', 'head'), may hold values from -0.119628906 to 0.119628906
- level_gain: float32 [16, 15, 80], P(None, None, 'head'), may hold values from 0.1 to 1
- level_code: int32 [512], P('seq'), may hold values from 0 to 15
Outputs:
- mixed: bfloat16 [32768, 5120], P('seq', 'head')
- grad_qk: float32 [32768, 128], P('seq')
- grad_values: bfloat16 [32768, 5120], P('seq', 'head')
Inputs may be any that keep to these rules, and one draw needn't show every extreme that they name: `level_code`: each span's row of the weight table.
All inputs are finite; a program needn't handle non-finite values.
Results may differ from a plain program's by a relative error of at most 0.005.
Values sent between devices are 32-bit elements; how exact they have to be, the bound alone decides.
No kernel may reach another device: no remote copies, remote signals or barrier semaphores. Data moves between devices by JAX's collectives and lax.ppermute only.
A program may use at most 128 MiB of HBM per device.

v0:
```python
import jax
import jax.numpy as jnp
from jax import lax
from jax.sharding import PartitionSpec as P

HEAD_DIM = 64
CH = 64
precise = lax.Precision.HIGHEST


def partner_2(value, axis, bit):
    mask = 2**bit
    pairs = [(source, source ^ mask) for source in range(lax.axis_size(axis))]
    return lax.ppermute(value, axis, pairs)


def bit_length(numbers, top_bits):
    bit_total = jnp.zeros_like(numbers)
    for bit_power in range(top_bits):
        bit_total = bit_total + (numbers >= 1 << bit_power).astype(jnp.int32)
    return bit_total


def local_levels(span_count):
    span_ids = jnp.arange(span_count, dtype=jnp.int32)
    return bit_length(span_ids[:, None] ^ span_ids[None, :], 8)


def local(query_key, values, cotangent, level_gain, level_code):
    tok_rows, state_dim = query_key.shape
    head_cols = values.shape[1]
    codes, levels, group_heads = level_gain.shape
    span_count = tok_rows // CH
    span_levels = span_count.bit_length() - 1
    seq_levels = lax.axis_size("seq").bit_length() - 1
    position = lax.axis_index("seq")
    picked = (level_code[:, None] == jnp.arange(codes, dtype=jnp.int32)[None, :]).astype(
        jnp.float32
    )
    level_weight = jnp.dot(
        picked, level_gain.reshape(codes, levels * group_heads), precision=precise
    ).reshape(span_count, levels, group_heads)
    cross_cols = jnp.repeat(
        level_weight[:, span_levels + 1 : span_levels + 1 + seq_levels, :], HEAD_DIM, axis=-1
    )
    own_state = lax.dot_general(
        query_key, values, (((0,), (0,)), ((), ())), preferred_element_type=jnp.float32
    )
    q_spans = query_key.reshape(span_count, CH, state_dim)
    c_spans = cotangent.reshape(span_count, CH, head_cols)
    span_grad = jnp.einsum("cti,ctj->cij", q_spans, c_spans, preferred_element_type=jnp.float32)
    level_grad = jnp.einsum("cij,clj->lij", span_grad, cross_cols, precision=precise)
    siblings = []
    adjoint = jnp.zeros_like(own_state)
    block_sum = own_state
    level_carry = level_grad
    for level_bit in range(seq_levels):
        partner = partner_2(block_sum, "seq", level_bit)
        upper_half = position >> level_bit & 1 == 1
        siblings.append(jnp.where(upper_half, partner, 0.0))
        block_sum = block_sum + partner
    for level_bit in range(seq_levels):
        partner_grad = partner_2(level_carry, "seq", level_bit)
        upper_half = position >> level_bit & 1 == 1
        adjoint = adjoint + jnp.where(upper_half, 0.0, partner_grad[0])
        level_carry = (level_carry + partner_grad)[1:]
    sibling = jnp.stack(siblings)
    span_state = jnp.einsum("clj,lij->cij", cross_cols, sibling, precision=precise).astype(
        jnp.bfloat16
    )
    adjoint_bf = adjoint.astype(jnp.bfloat16)
    scores = lax.dot_general(
        query_key, query_key, (((1,), (1,)), ((), ())), preferred_element_type=jnp.float32
    )
    onehot = (
        local_levels(span_count)[:, :, None]
        == jnp.arange(span_levels + 1, dtype=jnp.int32)[None, None, :]
    ).astype(jnp.float32)
    local_weight = jnp.einsum(
        "abk,akg->gab", onehot, level_weight[:, : span_levels + 1, :], precision=precise
    )
    causal = jnp.tril(jnp.ones((tok_rows, tok_rows), dtype=bool))
    pair_cols = 2 * HEAD_DIM

    def head_pair(pair_index, running):
        inner_out, dv_inner, d_score = running
        col_start = pair_index * pair_cols
        val_pair = lax.dynamic_slice_in_dim(values, col_start, pair_cols, 1).reshape(
            tok_rows, 2, HEAD_DIM
        )
        cot_pair = lax.dynamic_slice_in_dim(cotangent, col_start, pair_cols, 1).reshape(
            tok_rows, 2, HEAD_DIM
        )
        pair_weight = lax.dynamic_slice_in_dim(local_weight, pair_index * 2, 2, 0)
        weight = jnp.broadcast_to(
            pair_weight[:, :, None, :, None], (2, span_count, CH, span_count, CH)
        ).reshape(2, tok_rows, tok_rows)
        mixing = jnp.where(causal, weight * scores, 0.0).astype(jnp.bfloat16)
        part_out = jnp.einsum(
            "gts,sgp->tgp", mixing, val_pair, preferred_element_type=jnp.float32
        ).reshape(tok_rows, pair_cols)
        d_mix = jnp.einsum("tgp,sgp->gts", cot_pair, val_pair, preferred_element_type=jnp.float32)
        d_score = d_score + jnp.sum(jnp.where(causal, weight * d_mix, 0.0), axis=0)
        part_dv = jnp.einsum(
            "gts,tgp->sgp", mixing, cot_pair, preferred_element_type=jnp.float32
        ).reshape(tok_rows, pair_cols)
        inner_out = lax.dynamic_update_slice_in_dim(inner_out, part_out, col_start, 1)
        dv_inner = lax.dynamic_update_slice_in_dim(dv_inner, part_dv, col_start, 1)
        return (inner_out, dv_inner, d_score)

    start_state = (
        jnp.zeros((tok_rows, head_cols), jnp.float32),
        jnp.zeros((tok_rows, head_cols), jnp.float32),
        jnp.zeros((tok_rows, tok_rows), jnp.float32),
    )
    inner_out, dv_inner, d_score = lax.fori_loop(0, group_heads // 2, head_pair, start_state)
    outer_out = jnp.einsum(
        "cti,cij->ctj", q_spans, span_state, preferred_element_type=jnp.float32
    ).reshape(tok_rows, head_cols)
    mixed = (inner_out + outer_out).astype(jnp.bfloat16)
    dq_outer = jnp.einsum(
        "ctj,cij->cti", c_spans, span_state, preferred_element_type=jnp.float32
    ).reshape(tok_rows, state_dim)
    dv_outer = jnp.dot(query_key, adjoint_bf, preferred_element_type=jnp.float32)
    dk_outer = lax.dot_general(
        values, adjoint_bf, (((1,), (1,)), ((), ())), preferred_element_type=jnp.float32
    )
    q_float = query_key.astype(jnp.float32)
    dq_inner = jnp.dot(d_score, q_float, precision=precise) + lax.dot_general(
        d_score, q_float, (((0,), (0,)), ((), ())), precision=precise
    )
    head_part = dq_inner + dq_outer + dk_outer
    grad_qk = lax.psum(head_part, "head")
    grad_values = (dv_inner + dv_outer).astype(jnp.bfloat16)
    return (mixed, grad_qk, grad_values)


def solution(mesh):
    placed = (P("seq", None), P("seq", "head"), P("seq", "head"), P(None, None, "head"), P("seq"))
    return jax.shard_map(
        local,
        mesh=mesh,
        in_specs=placed,
        out_specs=(P("seq", "head"), P("seq", None), P("seq", "head")),
        check_vma=False,
    )
```

profile of v0, /device:TPU:2, one launch (start us, length us, event | category | flops | bytes accessed | tf_op | source)
XLA Modules:
  0.0 713.1 jit_solution(9387156875039487626)
XLA Ops:
  8.1 4.5 fusion.36
  12.6 6.3 copy.78
  19.9 2.7 copy-done.2
  24.0 10.4 %fusion.37 = f32[1280,6,128]{2,1,0:T(8,128)} fusion(f32[8,6,1280]{0,1,2:T(8,128)S(1)} %bitcast.108, f32[8,128,1280]{1,0,2:T(8,128)S(1)} %copy-done.4), kind=kOutput, calls=%fused_computation.70 | convolution fusion | flops 94371840 | bytes 9420800 | tf_op jit(solution)/shard_map/cij,clj->lij/dot_general | solution.py:52
  34.4 5.7 copy.79
  40.0 7.0 collective-permute-done.6
  47.0 3.8 slice_add_fusion
  53.2 71.2 %collective-permute-done.7 = f32[5,128,1280]{2,1,0:T(8,128)S(1)} collective-permute-done((f32[5,128,1280]{2,1,0:T(8,128)S(1)}, f32[5,128,1280]{2,1,0:T(8,128)S(1)}, u32[]{:S(2)}, u32[]{:S(2)}) %collective-permute-start.7) | collective-permute-done | bytes 3276832 | tf_op jit(solution)/shard_map/ppermute | solution.py:14
  135.8 64.5 %collective-permute-done.1 = f32[128,1280]{1,0:T(8,128)S(1)} collective-permute-done((f32[128,1280]{1,0:T(8,128)S(1)}, f32[128,1280]{1,0:T(8,128)S(1)}, u32[]{:S(2)}, u32[]{:S(2)}) %collective-permute-start.1) | collective-permute-done | bytes 655392 | tf_op jit(solution)/shard_map/ppermute | solution.py:14
  202.9 3.7 slice_add_fusion.2
  210.4 230.9 %while.19 = (s32[]{:T(128)}, f32[512,1280]{1,0:T(8,128)}, f32[512,1280]{0,1:T(8,128)}, f32[512,512]{1,0:T(8,128)}, bf16[512,1280]{1,0:T(8,128)(2,1)S(1)}, /*inde...) while((s32[]{:T(128)}, f32[512,1280]{1,0:T(8,128)}, ...), condition=%wide.region_2.3_spmd.clone.clone, body=%wide.region_0.2_spmd.clone.clone.sunk | while | flops 204996608 | bytes 29099832 | solution.py:116
  215.8 3.4 reshape.141
  238.0 3.4 reshape.141
  261.2 3.4 reshape.141
  284.4 3.4 reshape.141
  307.6 3.4 reshape.141
  330.8 3.4 reshape.141
  354.0 3.4 reshape.141
  377.1 3.4 reshape.141
  400.3 3.4 reshape.141
  423.5 3.4 reshape.141
  450.9 21.2 %collective-permute-done.3 = f32[128,1280]{1,0:T(8,128)S(1)} collective-permute-done((f32[128,1280]{1,0:T(8,128)S(1)}, f32[128,1280]{1,0:T(8,128)S(1)}, u32[]{:S(2)}, u32[]{:S(2)}) %collective-permute-start.3) | collective-permute-done | bytes 655392 | tf_op jit(solution)/shard_map/ppermute | solution.py:14
  474.1 59.5 %collective-permute-done.4 = f32[128,1280]{1,0:T(8,128)S(1)} collective-permute-done((f32[128,1280]{1,0:T(8,128)S(1)}, f32[128,1280]{1,0:T(8,128)S(1)}, u32[]{:S(2)}, u32[]{:S(2)}) %collective-permute-start.4) | collective-permute-done | bytes 655392 | tf_op jit(solution)/shard_map/ppermute | solution.py:14
  533.7 6.0 collective-permute-start.5
  541.9 34.5 %collective-permute-done.5 = f32[128,1280]{1,0:T(8,128)S(1)} collective-permute-done((f32[128,1280]{1,0:T(8,128)S(1)}, f32[128,1280]{1,0:T(8,128)S(1)}, u32[]{:S(2)}, u32[]{:S(2)}) %collective-permute-start.5) | collective-permute-done | bytes 655392 | tf_op jit(solution)/shard_map/ppermute | solution.py:14
  576.5 17.7 %collective-permute-done.11 = f32[1,128,1280]{2,1,0:T(8,128)S(1)} collective-permute-done((f32[1,128,1280]{2,1,0:T(8,128)S(1)}, f32[1,128,1280]{2,1,0:T(8,128)S(1)}, u32[]{:S(2)}, u32[]{:S(2)}) %collective-permute-start.11) | collective-permute-done | bytes 655392 | tf_op jit(solution)/shard_map/ppermute | solution.py:14
  594.2 3.0 fusion.9
  597.2 5.7 copy.73
  602.9 13.7 %convert_bitcast_fusion = bf16[8,128,1280]{1,0,2:T(8,128)(2,1)} fusion(f32[6,128,1280]{1,0,2:T(8,128)} %copy.73, f32[8,6,1280]{0,1,2:T(8,128)} %bitcast.109), kind=kOutput, calls=%fused_computation.17 | convolution fusion | flops 95682560 | bytes 6799360 | tf_op jit(solution)/shard_map/clj,lij->cij/dot_general | solution.py:68
  616.6 3.8 copy.75
  627.0 3.2 fusion.4
  632.3 72.3 %all-reduce.2.cloned.1.call-done = f32[512,128]{1,0:T(8,128)} async-done(((f32[512,128]{1,0:T(8,128)}), f32[512,128]{1,0:T(8,128)}) %all-reduce.2.cloned.1.call-update) | async-done | bytes 262160 | tf_op jit(solution)/shard_map/psum | solution.py:133
  (266 shorter events, 243.4 us)
Async XLA Ops:
  7.2 697.4 %all-reduce.2.cloned.1.call-start = ((), (), s32[]{:S(2)}) async-start(), calls=%async_computation | async-start | bytes 524288 | tf_op jit(solution)/shard_map/psum | solution.py:133
  12.6 6.3 copy-start.16
  12.6 6.6 copy-start.17
  19.6 4.4 copy-start.4
  19.9 2.7 copy-start.2
  40.0 7.0 collective-permute-start.6
  47.0 3.8 copy-start.10
  50.8 77.7 %copy-start.7 = (bf16[512,1280]{1,0:T(8,128)(2,1)S(1)}, bf16[512,1280]{1,0:T(8,128)(2,1)}, u32[]{:S(2)}) copy-start(bf16[512,1280]{1,0:T(8,128)(2,1)} %param.8) | copy-start | bytes 3932164
  50.8 73.6 %collective-permute-start.7 = (f32[5,128,1280]{2,1,0:T(8,128)S(1)}, f32[5,128,1280]{2,1,0:T(8,128)S(1)}, u32[]{:S(2)}, u32[]{:S(2)}) collective-permute-start(f32[5,128,1280]{2,1,0:T(8,128)S(1)} %slice_add_fusion), channel_id=1, source_target_pairs={{0,8},{4,12},{8,0},{12,4},{16,24},{20,28},{24,16},{28,20},{32,40},... | collective-permute-start | bytes 9830408 | tf_op jit(solution)/shard_map/ppermute | solution.py:14
  126.9 76.0 %collective-permute-start.8 = (f32[4,128,1280]{2,1,0:T(8,128)}, f32[4,128,1280]{2,1,0:T(8,128)}, u32[]{:S(2)}, u32[]{:S(2)}) collective-permute-start(f32[4,128,1280]{2,1,0:T(8,128)} %slice_add_fusion.1), channel_id=1, source_target_pairs={{0,16},{4,20},{8,24},{12,28},{16,0},{20,4},{24,8},{28,12},{32,48},... | collective-permute-start | bytes 7864328 | tf_op jit(solution)/shard_map/ppermute | solution.py:14
  128.9 2.2 collective-permute-start
  132.0 68.3 %collective-permute-start.1 = (f32[128,1280]{1,0:T(8,128)S(1)}, f32[128,1280]{1,0:T(8,128)S(1)}, u32[]{:S(2)}, u32[]{:S(2)}) collective-permute-start(f32[128,1280]{1,0:T(8,128)S(1)} %add.163), channel_id=1, source_target_pairs={{0,8},{4,12},{8,0},{12,4},{16,24},{20,28},{24,16},{28,20},{32,40},... | collective-permute-start | bytes 1966088 | tf_op jit(solution)/shard_map/ppermute | solution.py:14
  200.2 6.3 copy-start.12
  201.3 241.8 %collective-permute-start.2 = (f32[128,1280]{1,0:T(8,128)}, f32[128,1280]{1,0:T(8,128)}, u32[]{:S(2)}, u32[]{:S(2)}) collective-permute-start(f32[128,1280]{1,0:T(8,128)} %add.164), channel_id=1, source_target_pairs={{0,16},{4,20},{8,24},{12,28},{16,0},{20,4},{24,8},{28,12},{32,48},... | collective-permute-start | bytes 1966088 | tf_op jit(solution)/shard_map/ppermute | solution.py:14
  206.6 239.8 %collective-permute-start.9 = (f32[3,128,1280]{2,1,0:T(8,128)}, f32[3,128,1280]{2,1,0:T(8,128)}, u32[]{:S(2)}, u32[]{:S(2)}) collective-permute-start(f32[3,128,1280]{2,1,0:T(8,128)} %slice_add_fusion.2), channel_id=1, source_target_pairs={{0,32},{4,36},{8,40},{12,44},{16,48},{20,52},{24,56},{28,60},{32,0... | collective-permute-start | bytes 5898248 | tf_op jit(solution)/shard_map/ppermute | solution.py:14
  253.3 2.5 copy-start.8
  276.4 2.5 copy-start.8
  299.6 2.5 copy-start.8
  322.8 2.5 copy-start.8
  346.0 2.5 copy-start.8
  369.2 2.5 copy-start.8
  392.3 2.5 copy-start.8
  415.5 2.5 copy-start.8
  443.1 6.9 copy-start.15
  444.5 27.6 %collective-permute-start.3 = (f32[128,1280]{1,0:T(8,128)S(1)}, f32[128,1280]{1,0:T(8,128)S(1)}, u32[]{:S(2)}, u32[]{:S(2)}) collective-permute-start(f32[128,1280]{1,0:T(8,128)S(1)} %add.165), channel_id=1, source_target_pairs={{0,32},{4,36},{8,40},{12,44},{16,48},{20,52},{24,56},{28,60},{32,0... | collective-permute-start | bytes 1966088 | tf_op jit(solution)/shard_map/ppermute | solution.py:14
  448.2 24.1 %copy-start.13 = (f32[128,1280]{1,0:T(8,128)S(1)}, f32[128,1280]{1,0:T(8,128)}, u32[]{:S(2)}) copy-start(f32[128,1280]{1,0:T(8,128)} %copy-done.12) | copy-start | bytes 1966084
  448.2 91.6 %collective-permute-start.10 = (f32[2,128,1280]{2,1,0:T(8,128)S(1)}, f32[2,128,1280]{2,1,0:T(8,128)S(1)}, u32[]{:S(2)}, u32[]{:S(2)}) collective-permute-start(f32[2,128,1280]{2,1,0:T(8,128)S(1)} %slice_add_fusion.3), channel_id=1, source_target_pairs={{0,64},{4,68},{8,72},{12,76},{16,80},{20,84},{24,88},{28,92},{32,9... | collective-permute-start | bytes 3932168 | tf_op jit(solution)/shard_map/ppermute | solution.py:14
  472.2 61.5 %collective-permute-start.4 = (f32[128,1280]{1,0:T(8,128)S(1)}, f32[128,1280]{1,0:T(8,128)S(1)}, u32[]{:S(2)}, u32[]{:S(2)}) collective-permute-start(f32[128,1280]{1,0:T(8,128)S(1)} %add.166), channel_id=1, source_target_pairs={{0,64},{4,68},{8,72},{12,76},{16,80},{20,84},{24,88},{28,92},{32,9... | collective-permute-start | bytes 1966088 | tf_op jit(solution)/shard_map/ppermute | solution.py:14
  533.7 42.7 %collective-permute-start.5 = (f32[128,1280]{1,0:T(8,128)S(1)}, f32[128,1280]{1,0:T(8,128)S(1)}, u32[]{:S(2)}, u32[]{:S(2)}) collective-permute-start(f32[128,1280]{1,0:T(8,128)S(1)} %add.167), channel_id=1, source_target_pairs={{0,128},{4,132},{8,136},{12,140},{16,144},{20,148},{24,152},{28,15... | collective-permute-start | bytes 1966088 | tf_op jit(solution)/shard_map/ppermute | solution.py:14
  539.9 54.4 %collective-permute-start.11 = (f32[1,128,1280]{2,1,0:T(8,128)S(1)}, f32[1,128,1280]{2,1,0:T(8,128)S(1)}, u32[]{:S(2)}, u32[]{:S(2)}) collective-permute-start(f32[1,128,1280]{2,1,0:T(8,128)S(1)} %slice_add_fusion.4), channel_id=1, source_target_pairs={{0,128},{4,132},{8,136},{12,140},{16,144},{20,148},{24,152},{28,15... | collective-permute-start | bytes 1966088 | tf_op jit(solution)/shard_map/ppermute | solution.py:14
  622.8 3.0 copy-start.9
  627.0 3.2 copy-start.6
  (17 other events, 30.7 us)
Sparse Core Ops, SparseCore 0:
  627.1 77.3 all-reduce.1
where the time goes:
time: 717 us; the launch traced here: 713 us
  waiting for transfers between devices  350 us (49%)
  local copies, waits for them, and re-layouts  184 us (26%)
  matrix products  80 us (11%)
  other arithmetic  66.8 us (9%)
  starting transfers between devices  17.5 us (2%)
  between operations  14.3 us (2%)
    ppermute x12, waiting for transfers between devices, partner_2(): return lax.ppermute(value, axis, pairs)  278 us
    psum x1, waiting for transfers between devices, local(): grad_qk = lax.psum(head_part, 'head')  72.3 us
    dynamic_update_slice x20, local copies, waits for them, and re-layouts, head_pair(): lax.dynamic_update_slice_in_dim(inner_out, part_out, col_start, 1)  35 us
    reshape x10, local copies, waits for them, and re-layouts, head_pair(): weight = jnp.broadcast_to(pair_weight[:, :, None, :, None], (2, span_coun...  34.2 us
    dynamic_slice x20, local copies, waits for them, and re-layouts, head_pair(): lax.dynamic_slice_in_dim(cotangent, col_start, pair_cols, 1)  32.4 us
    broadcast_in_dim x10, local copies, waits for them, and re-layouts, head_pair(): jnp.broadcast_to(pair_weight[:, :, None, :, None], (2, span_count, CH, sp...  24 us
    add x10, other arithmetic, head_pair(): d_score = d_score + jnp.sum(jnp.where(causal, weight * d_mix, 0.0), axis=0)  23.9 us
    ppermute x12, starting transfers between devices, partner_2(): return lax.ppermute(value, axis, pairs)  17.5 us
  transfers between devices with their start and end apart: 13, of which 9 were waited for; matrix products, arithmetic and copies ran while one was open for 36% of the time, Pallas kernels for 0%

commit v1 on v0

--- a/solution.py
+++ b/solution.py
@@ -130,7 +130,8 @@
         d_score, q_float, (((0,), (0,)), ((), ())), precision=precise
     )
     head_part = dq_inner + dq_outer + dk_outer
-    grad_qk = lax.psum(head_part, "head")
+    pieces = lax.all_gather(head_part, "head", axis=0, tiled=False)
+    grad_qk = pieces.sum(axis=0)
     grad_values = (dv_inner + dv_outer).astype(jnp.bfloat16)
     return (mixed, grad_qk, grad_values)
 

time: 717 us -> 695 us (0.969)
  waiting for transfers between devices: 350 us -> 326 us
    psum x1 -> x0, waiting for transfers between devices: 72.3 us -> none  [local(): grad_qk = lax.psum(head_part, 'head')]
    all_gather x0 -> x1, waiting for transfers between devices: none -> 48.3 us  [local(): pieces = lax.all_gather(head_part, 'head', axis=0, tiled=False)]
  transfers between devices with their start and end apart: 13 -> 13, of which waited for: 9 -> 9; matrix products, arithmetic and copies ran while one was open for 36% -> 37% of each run, Pallas kernels for 0% -> 0%
where the time goes in v1:
time: 695 us; the launch traced here: 691 us
  waiting for transfers between devices  326 us (47%)
  local copies, waits for them, and re-layouts  184 us (26%)
  matrix products  81.4 us (12%)
  other arithmetic  67 us (10%)
  starting transfers between devices  17.5 us (3%)
  between operations  14.3 us (2%)
    ppermute x12, waiting for transfers between devices, partner_2(): return lax.ppermute(value, axis, pairs)  278 us
    all_gather x1, waiting for transfers between devices, local(): pieces = lax.all_gather(head_part, 'head', axis=0, tiled=False)  48.3 us
    dynamic_update_slice x20, local copies, waits for them, and re-layouts, head_pair(): lax.dynamic_update_slice_in_dim(inner_out, part_out, col_start, 1)  35 us
    reshape x10, local copies, waits for them, and re-layouts, head_pair(): weight = jnp.broadcast_to(pair_weight[:, :, None, :, None], (2, span_coun...  34.2 us
    dynamic_slice x20, local copies, waits for them, and re-layouts, head_pair(): lax.dynamic_slice_in_dim(cotangent, col_start, pair_cols, 1)  32.4 us
    broadcast_in_dim x10, local copies, waits for them, and re-layouts, head_pair(): jnp.broadcast_to(pair_weight[:, :, None, :, None], (2, span_count, CH, sp...  24 us
    add x10, other arithmetic, head_pair(): d_score = d_score + jnp.sum(jnp.where(causal, weight * d_mix, 0.0), axis=0)  23.9 us
    ppermute x12, starting transfers between devices, partner_2(): return lax.ppermute(value, axis, pairs)  17.5 us
  transfers between devices with their start and end apart: 13, of which 9 were waited for; matrix products, arithmetic and copies ran while one was open for 37% of the time, Pallas kernels for 0%

profile of v1, /device:TPU:2, one launch (start us, length us, event | category | flops | bytes accessed | tf_op | source)
XLA Modules:
  0.0 691.2 jit_solution(17752920025509780937)
XLA Ops:
  8.1 4.5 fusion.36
  12.6 6.3 copy.78
  19.9 2.7 copy-done.2
  24.0 10.3 %fusion.37 = f32[1280,6,128]{2,1,0:T(8,128)} fusion(f32[8,6,1280]{0,1,2:T(8,128)S(1)} %bitcast.109, f32[8,128,1280]{1,0,2:T(8,128)S(1)} %copy-done.4), kind=kOutput, calls=%fused_computation.70 | convolution fusion | flops 94371840 | bytes 9420800 | tf_op jit(solution)/shard_map/cij,clj->lij/dot_general | solution.py:52
  34.3 5.7 copy.79
  39.9 7.0 %collective-permute-done.6 = f32[6,128,1280]{2,1,0:T(8,128)S(1)} collective-permute-done((f32[6,128,1280]{2,1,0:T(8,128)}, f32[6,128,1280]{2,1,0:T(8,128)S(1)}, u32[]{:S(2)}, u32[]{:S(2)}) %collective-permute-start.6) | collective-permute-done | bytes 3932192 | tf_op jit(solution)/shard_map/ppermute | solution.py:14
  46.9 3.8 slice_add_fusion
  53.1 71.2 %collective-permute-done.7 = f32[5,128,1280]{2,1,0:T(8,128)S(1)} collective-permute-done((f32[5,128,1280]{2,1,0:T(8,128)S(1)}, f32[5,128,1280]{2,1,0:T(8,128)S(1)}, u32[]{:S(2)}, u32[]{:S(2)}) %collective-permute-start.7) | collective-permute-done | bytes 3276832 | tf_op jit(solution)/shard_map/ppermute | solution.py:14
  135.8 64.5 %collective-permute-done.1 = f32[128,1280]{1,0:T(8,128)S(1)} collective-permute-done((f32[128,1280]{1,0:T(8,128)S(1)}, f32[128,1280]{1,0:T(8,128)S(1)}, u32[]{:S(2)}, u32[]{:S(2)}) %collective-permute-start.1) | collective-permute-done | bytes 655392 | tf_op jit(solution)/shard_map/ppermute | solution.py:14
  202.9 3.7 slice_add_fusion.2
  210.3 230.8 %while.19 = (s32[]{:T(128)}, f32[512,1280]{1,0:T(8,128)}, f32[512,1280]{0,1:T(8,128)}, f32[512,512]{1,0:T(8,128)}, bf16[512,1280]{1,0:T(8,128)(2,1)S(1)}, /*inde...) while((s32[]{:T(128)}, f32[512,1280]{1,0:T(8,128)}, ...), condition=%wide.region_2.3_spmd.clone.clone, body=%wide.region_0.2_spmd.clone.clone.sunk | while | flops 204996608 | bytes 29099832 | solution.py:116
  215.8 3.4 reshape.142
  238.0 3.4 reshape.142
  261.2 3.4 reshape.142
  284.3 3.4 reshape.142
  307.5 3.4 reshape.142
  330.8 3.4 reshape.142
  353.9 3.4 reshape.142
  377.1 3.4 reshape.142
  400.3 3.4 reshape.142
  423.4 3.4 reshape.142
  450.7 21.2 %collective-permute-done.3 = f32[128,1280]{1,0:T(8,128)S(1)} collective-permute-done((f32[128,1280]{1,0:T(8,128)S(1)}, f32[128,1280]{1,0:T(8,128)S(1)}, u32[]{:S(2)}, u32[]{:S(2)}) %collective-permute-start.3) | collective-permute-done | bytes 655392 | tf_op jit(solution)/shard_map/ppermute | solution.py:14
  474.0 59.5 %collective-permute-done.4 = f32[128,1280]{1,0:T(8,128)S(1)} collective-permute-done((f32[128,1280]{1,0:T(8,128)S(1)}, f32[128,1280]{1,0:T(8,128)S(1)}, u32[]{:S(2)}, u32[]{:S(2)}) %collective-permute-start.4) | collective-permute-done | bytes 655392 | tf_op jit(solution)/shard_map/ppermute | solution.py:14
  533.6 6.0 collective-permute-start.5
  541.8 34.5 %collective-permute-done.5 = f32[128,1280]{1,0:T(8,128)S(1)} collective-permute-done((f32[128,1280]{1,0:T(8,128)S(1)}, f32[128,1280]{1,0:T(8,128)S(1)}, u32[]{:S(2)}, u32[]{:S(2)}) %collective-permute-start.5) | collective-permute-done | bytes 655392 | tf_op jit(solution)/shard_map/ppermute | solution.py:14
  576.3 17.7 %collective-permute-done.11 = f32[1,128,1280]{2,1,0:T(8,128)S(1)} collective-permute-done((f32[1,128,1280]{2,1,0:T(8,128)S(1)}, f32[1,128,1280]{2,1,0:T(8,128)S(1)}, u32[]{:S(2)}, u32[]{:S(2)}) %collective-permute-start.11) | collective-permute-done | bytes 655392 | tf_op jit(solution)/shard_map/ppermute | solution.py:14
  594.1 3.0 fusion.9
  597.0 5.7 copy.73
  602.8 13.7 %convert_bitcast_fusion = bf16[8,128,1280]{1,0,2:T(8,128)(2,1)} fusion(f32[6,128,1280]{1,0,2:T(8,128)} %copy.73, f32[8,6,1280]{0,1,2:T(8,128)} %bitcast.110), kind=kOutput, calls=%fused_computation.17 | convolution fusion | flops 95682560 | bytes 6799360 | tf_op jit(solution)/shard_map/clj,lij->cij/dot_general | solution.py:68
  616.5 3.8 copy.75
  625.1 3.3 fusion.3
  634.0 48.3 %all-gather.3.cloned.1.call-done = f32[2048,128]{1,0:T(8,128)} async-done(((f32[512,128]{1,0:T(8,128)}), f32[2048,128]{1,0:T(8,128)}) %all-gather.3.cloned.1.call-update) | async-done | bytes 1048592 | tf_op jit(solution)/shard_map/all_gather | solution.py:133
  (264 shorter events, 245.5 us)
Async XLA Ops:
  7.2 675.1 %all-gather.3.cloned.1.call-start = ((), (), s32[]{:S(2)}) async-start(), calls=%async_computation | async-start | bytes 1310720 | tf_op jit(solution)/shard_map/all_gather | solution.py:133
  12.6 6.3 copy-start.15
  12.6 6.6 copy-start.16
  19.6 4.4 copy-start.4
  19.9 2.7 copy-start.2
  39.9 7.0 %collective-permute-start.6 = (f32[6,128,1280]{2,1,0:T(8,128)}, f32[6,128,1280]{2,1,0:T(8,128)S(1)}, u32[]{:S(2)}, u32[]{:S(2)}) collective-permute-start(f32[6,128,1280]{2,1,0:T(8,128)} %bitcast.117), channel_id=1, source_target_pairs={{0,4},{4,0},{8,12},{12,8},{16,20},{20,16},{24,28},{28,24},{32,36},... | collective-permute-start | bytes 11796488 | tf_op jit(solution)/shard_map/ppermute | solution.py:14
  46.9 3.8 copy-start.9
  50.7 77.8 %copy-start.6 = (bf16[512,1280]{1,0:T(8,128)(2,1)S(1)}, bf16[512,1280]{1,0:T(8,128)(2,1)}, u32[]{:S(2)}) copy-start(bf16[512,1280]{1,0:T(8,128)(2,1)} %param.8) | copy-start | bytes 3932164
  50.7 73.6 %collective-permute-start.7 = (f32[5,128,1280]{2,1,0:T(8,128)S(1)}, f32[5,128,1280]{2,1,0:T(8,128)S(1)}, u32[]{:S(2)}, u32[]{:S(2)}) collective-permute-start(f32[5,128,1280]{2,1,0:T(8,128)S(1)} %slice_add_fusion), channel_id=1, source_target_pairs={{0,8},{4,12},{8,0},{12,4},{16,24},{20,28},{24,16},{28,20},{32,40},... | collective-permute-start | bytes 9830408 | tf_op jit(solution)/shard_map/ppermute | solution.py:14
  124.3 2.6 copy-start.10
  126.9 76.0 %collective-permute-start.8 = (f32[4,128,1280]{2,1,0:T(8,128)}, f32[4,128,1280]{2,1,0:T(8,128)}, u32[]{:S(2)}, u32[]{:S(2)}) collective-permute-start(f32[4,128,1280]{2,1,0:T(8,128)} %slice_add_fusion.1), channel_id=1, source_target_pairs={{0,16},{4,20},{8,24},{12,28},{16,0},{20,4},{24,8},{28,12},{32,48},... | collective-permute-start | bytes 7864328 | tf_op jit(solution)/shard_map/ppermute | solution.py:14
  128.9 2.2 collective-permute-start
  132.0 68.3 %collective-permute-start.1 = (f32[128,1280]{1,0:T(8,128)S(1)}, f32[128,1280]{1,0:T(8,128)S(1)}, u32[]{:S(2)}, u32[]{:S(2)}) collective-permute-start(f32[128,1280]{1,0:T(8,128)S(1)} %add.161), channel_id=1, source_target_pairs={{0,8},{4,12},{8,0},{12,4},{16,24},{20,28},{24,16},{28,20},{32,40},... | collective-permute-start | bytes 1966088 | tf_op jit(solution)/shard_map/ppermute | solution.py:14
  200.2 6.4 copy-start.11
  201.3 241.7 %collective-permute-start.2 = (f32[128,1280]{1,0:T(8,128)}, f32[128,1280]{1,0:T(8,128)}, u32[]{:S(2)}, u32[]{:S(2)}) collective-permute-start(f32[128,1280]{1,0:T(8,128)} %add.162), channel_id=1, source_target_pairs={{0,16},{4,20},{8,24},{12,28},{16,0},{20,4},{24,8},{28,12},{32,48},... | collective-permute-start | bytes 1966088 | tf_op jit(solution)/shard_map/ppermute | solution.py:14
  206.6 239.6 %collective-permute-start.9 = (f32[3,128,1280]{2,1,0:T(8,128)}, f32[3,128,1280]{2,1,0:T(8,128)}, u32[]{:S(2)}, u32[]{:S(2)}) collective-permute-start(f32[3,128,1280]{2,1,0:T(8,128)} %slice_add_fusion.2), channel_id=1, source_target_pairs={{0,32},{4,36},{8,40},{12,44},{16,48},{20,52},{24,56},{28,60},{32,0... | collective-permute-start | bytes 5898248 | tf_op jit(solution)/shard_map/ppermute | solution.py:14
  253.2 2.5 copy-start.7
  276.3 2.5 copy-start.7
  299.6 2.5 copy-start.7
  322.8 2.5 copy-start.7
  345.9 2.5 copy-start.7
  369.1 2.5 copy-start.7
  392.3 2.5 copy-start.7
  415.4 2.5 copy-start.7
  442.9 6.9 copy-start.14
  444.4 27.6 %collective-permute-start.3 = (f32[128,1280]{1,0:T(8,128)S(1)}, f32[128,1280]{1,0:T(8,128)S(1)}, u32[]{:S(2)}, u32[]{:S(2)}) collective-permute-start(f32[128,1280]{1,0:T(8,128)S(1)} %add.163), channel_id=1, source_target_pairs={{0,32},{4,36},{8,40},{12,44},{16,48},{20,52},{24,56},{28,60},{32,0... | collective-permute-start | bytes 1966088 | tf_op jit(solution)/shard_map/ppermute | solution.py:14
  448.1 24.1 %copy-start.12 = (f32[128,1280]{1,0:T(8,128)S(1)}, f32[128,1280]{1,0:T(8,128)}, u32[]{:S(2)}) copy-start(f32[128,1280]{1,0:T(8,128)} %copy-done.11) | copy-start | bytes 1966084
  448.1 91.6 %collective-permute-start.10 = (f32[2,128,1280]{2,1,0:T(8,128)S(1)}, f32[2,128,1280]{2,1,0:T(8,128)S(1)}, u32[]{:S(2)}, u32[]{:S(2)}) collective-permute-start(f32[2,128,1280]{2,1,0:T(8,128)S(1)} %slice_add_fusion.3), channel_id=1, source_target_pairs={{0,64},{4,68},{8,72},{12,76},{16,80},{20,84},{24,88},{28,92},{32,9... | collective-permute-start | bytes 3932168 | tf_op jit(solution)/shard_map/ppermute | solution.py:14
  472.1 61.5 %collective-permute-start.4 = (f32[128,1280]{1,0:T(8,128)S(1)}, f32[128,1280]{1,0:T(8,128)S(1)}, u32[]{:S(2)}, u32[]{:S(2)}) collective-permute-start(f32[128,1280]{1,0:T(8,128)S(1)} %add.164), channel_id=1, source_target_pairs={{0,64},{4,68},{8,72},{12,76},{16,80},{20,84},{24,88},{28,92},{32,9... | collective-permute-start | bytes 1966088 | tf_op jit(solution)/shard_map/ppermute | solution.py:14
  533.6 42.7 %collective-permute-start.5 = (f32[128,1280]{1,0:T(8,128)S(1)}, f32[128,1280]{1,0:T(8,128)S(1)}, u32[]{:S(2)}, u32[]{:S(2)}) collective-permute-start(f32[128,1280]{1,0:T(8,128)S(1)} %add.165), channel_id=1, source_target_pairs={{0,128},{4,132},{8,136},{12,140},{16,144},{20,148},{24,152},{28,15... | collective-permute-start | bytes 1966088 | tf_op jit(solution)/shard_map/ppermute | solution.py:14
  539.7 54.4 %collective-permute-start.11 = (f32[1,128,1280]{2,1,0:T(8,128)S(1)}, f32[1,128,1280]{2,1,0:T(8,128)S(1)}, u32[]{:S(2)}, u32[]{:S(2)}) collective-permute-start(f32[1,128,1280]{2,1,0:T(8,128)S(1)} %slice_add_fusion.4), channel_id=1, source_target_pairs={{0,128},{4,132},{8,136},{12,140},{16,144},{20,148},{24,152},{28,15... | collective-permute-start | bytes 1966088 | tf_op jit(solution)/shard_map/ppermute | solution.py:14
  620.3 3.5 copy-start.8
  (16 other events, 28.1 us)
Sparse Core Ops, SparseCore 0:
  625.2 57.0 all-gather.2
